TPU v7x, 128 devices: a whole 4x4x4 slice. The times are simulated.
128 devices in a mesh: img: 8 (over z, core), txt: 16 (over y, x).
Axes of the slice: x: 4, y: 4, z: 4, core: 2. Of those that a mesh axis runs over, the one named last changes fastest.
Arguments:
- photo_embedding_raw: bfloat16 [16384, 1152], P(('img', 'txt')), may hold values from -4 to 4
- sentence_embedding_raw: bfloat16 [16384, 1152], P(('txt', 'img')), may hold values from -4 to 4
- photo_match_ids: int32 [16384], P(('img', 'txt')), may hold values from 0 to 16383
- sentence_match_ids: int32 [16384], P(('txt', 'img')), may hold values from 0 to 16383
- sharpness_array: float32 [1], replicated, may hold values from 20 to 40
- offset_term_array: float32 [1], replicated, may hold values from -8 to -6
Outputs:
- image_grad: float32 [16384, 1152], P(('img', 'txt'))
- text_grad: float32 [16384, 1152], P(('txt', 'img'))
- loss: float32 [1], replicated
All inputs are finite; a program needn't handle non-finite values.
Results may differ from a plain program's by a relative error of at most 0.0054.
Values may be sent and summed in bfloat16 or wider, within the bound.
A program may use at most 64 MiB of HBM per device.

v0:
```python
import jax
import jax.numpy as jnp
from jax import lax
from jax.sharding import PartitionSpec as P

epsilon = 1e-06


def normalize(values):
    wide = values.astype(jnp.float32)
    inverse = lax.rsqrt(jnp.sum(wide * wide, axis=-1, keepdims=True) + epsilon)
    return (wide * inverse, inverse)


def score_block(picture_row_slice, row_ids, text_rows, column_ids, sharpness_multiplier, offset):
    pair_scores = (
        sharpness_multiplier
        * lax.dot_general(
            picture_row_slice,
            text_rows,
            (((1,), (1,)), ((), ())),
            preferred_element_type=jnp.float32,
        )
        + offset
    )
    positive = (row_ids[:, None] == column_ids[None, :]).astype(jnp.float32)
    signed = 2.0 * positive - 1.0
    share = jnp.sum(jax.nn.softplus(-signed * pair_scores))
    pair_coef = (sharpness_multiplier * (jax.nn.sigmoid(pair_scores) - positive)).astype(
        jnp.bfloat16
    )
    return (pair_coef, share)


def transpose_product(pair_coef, picture_row_slice):
    return lax.dot_general(
        pair_coef, picture_row_slice, (((0,), (0,)), ((), ())), preferred_element_type=jnp.float32
    )


def backward_norm(unit_rows, inverse, direction):
    along = jnp.sum(unit_rows * direction, axis=-1, keepdims=True)
    return inverse * (direction - unit_rows * along)


def on_device(
    photo_embedding_raw,
    sentence_embedding_raw,
    photo_match_ids,
    sentence_match_ids,
    sharpness_array,
    offset_term_array,
):
    sharpness_multiplier = sharpness_array[0]
    offset = offset_term_array[0]
    image_unit, image_inverse = normalize(photo_embedding_raw)
    text_unit, text_inverse = normalize(sentence_embedding_raw)
    image_send = image_unit.astype(jnp.bfloat16)
    text_send = text_unit.astype(jnp.bfloat16)
    images_all, row_ids_all = (
        lax.all_gather(image_send, "txt", axis=0, tiled=True),
        lax.all_gather(photo_match_ids, "txt", axis=0, tiled=True),
    )
    text_rows = lax.all_gather(text_send, "img", axis=0, tiled=True)
    column_ids = lax.all_gather(sentence_match_ids, "img", axis=0, tiled=True)
    pair_coef, share = score_block(
        images_all, row_ids_all, text_rows, column_ids, sharpness_multiplier, offset
    )
    image_acc = jnp.dot(pair_coef, text_rows, preferred_element_type=jnp.float32)
    text_acc = transpose_product(pair_coef, images_all)
    text_dir = lax.psum_scatter(text_acc, "img", scatter_dimension=0, tiled=True)
    image_dir = lax.psum_scatter(image_acc, "txt", scatter_dimension=0, tiled=True)
    summed_loss_value = lax.psum(share, ("img", "txt"))
    batch_total = photo_embedding_raw.shape[0] * lax.axis_size("img") * lax.axis_size("txt")
    image_grad = backward_norm(image_unit, image_inverse, image_dir)
    text_grad = backward_norm(text_unit, text_inverse, text_dir)
    loss = (summed_loss_value / batch_total).reshape(1)
    return (image_grad, text_grad, loss)


def solution(mesh):
    return jax.shard_map(
        on_device,
        mesh=mesh,
        in_specs=(
            P(("img", "txt"), None),
            P(("txt", "img"), None),
            P(("img", "txt")),
            P(("txt", "img")),
            P(),
            P(),
        ),
        out_specs=(P(("img", "txt"), None), P(("txt", "img"), None), P()),
        check_vma=False,
    )
```

profile of v0, /device:TPU:1, one launch (start us, length us, event | category | flops | bytes accessed | tf_op | source)
XLA Modules:
  0.0 261.7 jit_solution(1261813103426942824)
XLA Ops:
  7.2 0.0 all-gather.7.cloned.1.call-start
  7.2 1.1 fusion.20
  8.3 1.8 fusion.9
  10.1 0.0 all-gather.7.cloned.1.call-update
  10.1 0.0 all-gather.5.cloned.1.call-start
  10.2 1.1 fusion.16
  11.3 1.8 fusion.12
  13.1 0.0 reduce-scatter.5.cloned.1.call-start
  14.5 13.2 %all-gather.1 = s32[8,1,128]{2,1,0:T(1,128)S(1)} all-gather(s32[1,1,128]{2,1,0:T(1,128)} %bitcast.17), channel_id=1, replica_groups=mesh['img'=8,'txt'=16] {'img'}, dimensions={0}, use_global_device_ids=true | all-gather | bytes 4608 | tf_op jit(solution)/shard_map/all_gather | solution.py:65
  27.7 17.6 %all-gather = s32[16,1,128]{2,1,0:T(1,128)S(1)} all-gather(s32[1,1,128]{2,1,0:T(1,128)} %bitcast.18), channel_id=1, replica_groups=mesh['img'=8,'txt'=16] {'txt'}, dimensions={0}, use_global_device_ids=true | all-gather | bytes 8704 | tf_op jit(solution)/shard_map/all_gather | solution.py:62
  45.3 51.1 %all-gather.5.cloned.1.call-done = bf16[2048,1152]{1,0:T(8,128)(2,1)} async-done(((bf16[128,1152]{1,0:T(8,128)(2,1)}), bf16[2048,1152]{1,0:T(8,128)(2,1)}) %all-gather.5.cloned.1.call-update) | async-done | bytes 4718608 | tf_op jit(solution)/shard_map/all_gather | solution.py:61
  96.4 16.3 %fusion.6 = (f32[]{:T(128)}, bf16[2048,1024]{1,0:T(8,128)(2,1)S(1)}) fusion(s32[1024]{0:T(1024)S(1)} %bitcast.16, f32[]{:T(128)} %bitcast.14, f32[]{:T(128)} %bitcast.13, s32[2048]{0:T(1024)S(1)} %bitcast.15, bf16[2048,1152]{1,0:T(8,128)(2,1)} %all-gather.5.cloned.1.call-done, bf16[1024,1152]{1,0:T(8,128)(2,1)} %all-gather.7.cloned.1.call-done), kind=kOutput, calls=%fused_computation.9 | convolution fusion | flops 4875878400 | bytes 11284492 | tf_op jit(solution)/shard_map/dot_general | solution.py:18
  112.7 1.9 copy-done.4
  114.6 7.6 %fusion.22 = f32[1024,1152]{1,0:T(8,128)} fusion(bf16[2048,1024]{1,0:T(8,128)(2,1)S(1)} %get-tuple-element.4, bf16[2048,1152]{1,0:T(8,128)(2,1)S(1)} %copy-done.2), kind=kOutput, calls=%fused_computation.32 | convolution fusion | flops 4831838208 | bytes 13631488 | tf_op jit(solution)/shard_map/dot_general | solution.py:36
  122.2 0.0 reduce-scatter.3.cloned.1.call-start
  122.3 9.6 %fusion.21 = f32[2048,1152]{1,0:T(8,128)} fusion(bf16[2048,1024]{1,0:T(8,128)(2,1)} %copy-done.4, bf16[1024,1152]{1,0:T(8,128)(2,1)S(1)} %copy-done.3), kind=kOutput, calls=%fused_computation.31 | convolution fusion | flops 4831838208 | bytes 15990784 | tf_op jit(solution)/shard_map/dot_general | solution.py:69
  131.8 0.0 reduce-scatter.3.cloned.1.call-update
  131.9 66.0 %psum.7 = f32[]{:T(128)} all-reduce(f32[]{:T(128)} %get-tuple-element.3), channel_id=1, replica_groups=mesh['img'=8,'txt'=16] {'img','txt'}, use_global_device_ids=true, to_apply=%region_7.8 | all-reduce | flops 1 | bytes 8 | tf_op jit(solution)/shard_map/psum | solution.py:73
  198.6 0.0 reduce-scatter.5.cloned.1.call-done
  198.6 1.3 fusion.17
  199.9 2.1 fusion.19
  202.0 48.6 %reduce-scatter.3.cloned.1.call-done = f32[128,1152]{1,0:T(8,128)} async-done(((f32[2048,1152]{1,0:T(8,128)}), f32[128,1152]{1,0:T(8,128)}) %reduce-scatter.3.cloned.1.call-update) | async-done | bytes 589840 | tf_op jit(solution)/shard_map/reduce_scatter | solution.py:72
  250.7 1.3 fusion.13
  252.0 2.1 fusion.15
  (14 shorter events, 0.1 us)
Async XLA Ops:
  7.2 38.1 %all-gather.7.cloned.1.call-start = ((), (), s32[]{:S(2)}) async-start(), calls=%async_computation.3 | async-start | bytes 2654208 | tf_op jit(solution)/shard_map/all_gather | solution.py:64
  10.1 86.2 %all-gather.5.cloned.1.call-start = ((), (), s32[]{:S(2)}) async-start(), calls=%async_computation.2 | async-start | bytes 5013504 | tf_op jit(solution)/shard_map/all_gather | solution.py:61
  13.1 185.5 %reduce-scatter.5.cloned.1.call-start = ((), (), s32[]{:S(2)}) async-start(), calls=%async_computation.5 | async-start | bytes 5308416 | tf_op jit(solution)/shard_map/reduce_scatter | solution.py:71
  96.4 18.3 %copy-start.2 = (bf16[2048,1152]{1,0:T(8,128)(2,1)S(1)}, bf16[2048,1152]{1,0:T(8,128)(2,1)}, u32[]{:S(2)}) copy-start(bf16[2048,1152]{1,0:T(8,128)(2,1)} %all-gather.5.cloned.1.call-done) | copy-start | bytes 14155780
  112.7 1.9 copy-start.4
  114.6 7.6 %copy-start.3 = (bf16[1024,1152]{1,0:T(8,128)(2,1)S(1)}, bf16[1024,1152]{1,0:T(8,128)(2,1)}, u32[]{:S(2)}) copy-start(bf16[1024,1152]{1,0:T(8,128)(2,1)} %all-gather.7.cloned.1.call-done) | copy-start | bytes 7077892
  122.2 128.5 %reduce-scatter.3.cloned.1.call-start = ((), (), s32[]{:S(2)}) async-start(), calls=%async_computation.4 | async-start | bytes 10027008 | tf_op jit(solution)/shard_map/reduce_scatter | solution.py:72
  131.8 66.8 %copy-start = (bf16[128,1152]{1,0:T(8,128)(2,1)S(1)}, bf16[128,1152]{1,0:T(8,128)(2,1)}, u32[]{:S(2)}) copy-start(bf16[128,1152]{1,0:T(8,128)(2,1)} %param.7) | copy-start | bytes 884740
  131.8 118.8 %copy-start.1 = (bf16[128,1152]{1,0:T(8,128)(2,1)S(1)}, bf16[128,1152]{1,0:T(8,128)(2,1)}, u32[]{:S(2)}) copy-start(bf16[128,1152]{1,0:T(8,128)(2,1)} %param.6) | copy-start | bytes 884740
Sparse Core Ops, SparseCore 0:
  10.3 29.4 all-gather.6
  42.5 53.8 all-gather.4
  122.3 36.5 reduce-scatter.4
  162.3 88.3 reduce-scatter.2
where the time goes:
time: 263 us; the launch traced here: 262 us
  waiting for transfers between devices  99.8 us (38%)
  blocking collectives  96.9 us (37%)
  matrix products  33.4 us (13%)
  between operations  16.9 us (6%)
  other arithmetic  12.6 us (5%)
    psum x1, blocking collectives, on_device(): summed_loss_value = lax.psum(share, ('img', 'txt'))  66 us
    all_gather x1, waiting for transfers between devices, on_device(): lax.all_gather(image_send, 'txt', axis=0, tiled=True)  51.1 us
    reduce_scatter x1, waiting for transfers between devices, on_device(): lax.psum_scatter(image_acc, 'txt', scatter_dimension=0, tiled=True)  48.6 us
    all_gather x1, blocking collectives, on_device(): lax.all_gather(photo_match_ids, 'txt', axis=0, tiled=True)  17.6 us
    dot_general x1, matrix products, score_block(): lax.dot_general(picture_row_slice, text_rows, (((1,), (1,)), ((), ())), p...  16.3 us
    all_gather x1, blocking collectives, on_device(): column_ids = lax.all_gather(sentence_match_ids, 'img', axis=0, tiled=True)  13.2 us
    dot_general x1, matrix products, on_device(): jnp.dot(pair_coef, text_rows, preferred_element_type=jnp.float32)  9.56 us
    dot_general x1, matrix products, transpose_product(): lax.dot_general(pair_coef, picture_row_slice, (((0,), (0,)), ((), ())), p...  7.55 us
  transfers between devices with their start and end apart: 4, of which 2 were waited for; matrix products, arithmetic and copies ran while one was open for 6% of the time, Pallas kernels for 0%

commit v1 on v0

v1 whole, which is shorter than its diff:
```python
import functools

import jax
import jax.numpy as jnp
from jax import lax
from jax.experimental import pallas as pl
from jax.experimental.pallas import tpu as pltpu
from jax.sharding import PartitionSpec as P

MESH = pl.DeviceIdType.MESH
EPSILON = 1e-06
D = 1152
ROWS = 128
BATCH = 16384
F32 = jnp.float32
BF16 = jnp.bfloat16

POS = {(0, 0): 0, (0, 1): 1, (0, 3): 2, (1, 0): 3, (1, 1): 4, (0, 2): 5, (1, 3): 6, (1, 2): 7}
SENDS = {
    "R": [(0, 0, 64, 128), (0, 0, 0, 64), (1, 0, 0, 64), (0, 3, 64, 128), (1, 3, 0, 64)],
    "L": [(0, 0, 64, 128), (0, 0, 0, 64), (1, 0, 0, 64), (0, 1, 0, 64), (1, 1, 64, 128)],
    "V": [(0, 0, 0, 64), (0, 0, 64, 128), (0, 1, 64, 128), (0, 3, 64, 128)],
}
EVENTS = [(k, link) for k in range(5) for link in "RLV" if k < len(SENDS[link])]
INDEX = {event: i for i, event in enumerate(EVENTS)}
BACK = {"R": "L", "L": "R", "V": "V"}
RETURNS = [
    [(4, "R"), (4, "L"), (3, "V")],
    [(3, "R"), (3, "L")],
    [(2, "R"), (2, "L"), (2, "V")],
    [(1, "R"), (1, "L"), (1, "V")],
    [(0, "R"), (0, "L"), (0, "V")],
]
SIDES = "xy"
ROW_TILE = 512
COL_TILE = 256
SLICE = 16


def landing(link, entry):
    pair, offset, first, last = entry
    if link == "R":
        return (pair, (offset + 3) % 4, first, last)
    if link == "L":
        return (pair, (offset + 1) % 4, first, last)
    return (1 - pair, offset, first, last)


def partners():
    i = lax.axis_index("img")
    t = lax.axis_index("txt")
    z, c, y, x = i // 2, i % 2, t // 4, t % 4

    def at(x, y, z, c):
        return (z * 2 + c, y * 4 + x)

    return {
        "xR": at((x + 1) % 4, y, z, c),
        "xL": at((x + 3) % 4, y, z, c),
        "xV": at(x, y, z + 1 - 2 * (z % 2), c),
        "x2": at((x + 2) % 4, y, z, c),
        "yR": at(x, (y + 1) % 4, z, c),
        "yL": at(x, (y + 3) % 4, z, c),
        "yV": at(x, y, 3 - z, c),
        "y2": at(x, (y + 2) % 4, z, c),
        "sib": at(x, y, z, 1 - c),
        "x1": at(x + 1 - 2 * (x % 2), y, z, c),
        "y1": at(x, y + 1 - 2 * (y % 2), z, c),
    }


BARRIER = ("xR", "xL", "xV", "x2", "yR", "yL", "yV", "y2", "sib")
LOSS_STEPS = ("x1", "x2", "y1", "y2", "xV", "yV", "sib")


def normalize(values):
    wide = values.astype(F32)
    inverse = lax.rsqrt(jnp.sum(wide * wide, axis=-1, keepdims=True) + EPSILON)
    return wide * inverse, inverse


def kernel(
    img_raw, txt_raw, img_ids, txt_ids, sharp_ref, offset_ref,
    img_out, txt_out, loss_out,
    images, texts, coef, coef_t, score0, score1, row_ids, col_ids, img_part, txt_part, loss_acc,
    sib_send, sib_recv, back_send, back_recv, idx, idt, loss_send, loss_recv,
    g_ss, g_rs, f_ss, f_rs, b_ss, b_rs, p_ss, p_rs, i_ss, i_rs, l_ss, l_rs,
):
    to = partners()
    sharp = sharp_ref[0]
    offset = offset_ref[0]
    raw = {"x": img_raw, "y": txt_raw}

    def remote(src, dst, send, recv, where):
        return pltpu.make_async_remote_copy(
            src_ref=src, dst_ref=dst, send_sem=send, recv_sem=recv, device_id=to[where], device_id_type=MESH
        )

    pending = []

    def start(copy):
        copy.start()
        pending.append(copy)

    barrier = pltpu.get_barrier_semaphore()
    for name in BARRIER:
        pl.semaphore_signal(barrier, inc=1, device_id=to[name], device_id_type=MESH)
    images[0:ROWS, :] = normalize(img_raw[...])[0].astype(BF16)
    texts[0:ROWS, :] = normalize(txt_raw[...])[0].astype(BF16)
    idx[0, 0, 0] = img_ids[...]
    idt[0, 0] = txt_ids[...]
    pl.semaphore_wait(barrier, len(BARRIER))

    def rows_of(side, entry):
        pair, off, first, last = entry
        pos = POS[(pair, off)]
        if side == "x":
            return images.at[pl.ds(pos * 256 + first, last - first)]
        return texts.at[pl.ds(pos * 128 + first, last - first)]

    gather = {}
    for side in SIDES:
        for event in EVENTS:
            k, link = event
            n = INDEX[event] + (0 if side == "x" else len(EVENTS))
            entry = SENDS[link][k]
            gather[side, event] = remote(
                rows_of(side, entry), rows_of(side, landing(link, entry)), g_ss.at[n], g_rs.at[n], side + link
            )

    forwards = {}

    def forward(entry):
        n = sum(len(copies) for copies in forwards.values())
        pair, off, first, last = entry
        at = POS[(pair, off)] * 256 + first
        copy = remote(
            images.at[pl.ds(at, last - first)], images.at[pl.ds(at + 128, last - first)], f_ss.at[n], f_rs.at[n], "sib"
        )
        start(copy)
        forwards.setdefault(POS[(pair, off)], []).append(copy)

    def send_slot(k):
        for event in EVENTS:
            if event[0] == k:
                for side in SIDES:
                    start(gather[side, event])

    def receive_slot(k):
        for event in EVENTS:
            if event[0] == k:
                for side in SIDES:
                    gather[side, event].wait_recv()
                forward(landing(event[1], SENDS[event[1]][k]))

    def receive_sibling(*positions):
        for pos in positions:
            for copy in forwards[pos]:
                copy.wait_recv()

    send_slot(0)
    send_slot(1)
    id_copies = {}
    for n, (where, slot) in enumerate((("R", 3), ("L", 1), ("2", 2))):
        id_copies["x", n] = remote(idx.at[0, 0, 0], idx.at[0, 0, slot], i_ss.at[n], i_rs.at[n], "x" + where)
        id_copies["y", n] = remote(idt.at[0, 0], idt.at[0, slot], i_ss.at[3 + n], i_rs.at[3 + n], "y" + where)
    id_copies["x", 3] = remote(idx.at[0, 0], idx.at[0, 1], i_ss.at[6], i_rs.at[6], "xV")
    id_copies["y", 3] = remote(idt.at[0], idt.at[1], i_ss.at[7], i_rs.at[7], "yV")
    id_copies["x", 4] = remote(idx.at[0], idx.at[1], i_ss.at[8], i_rs.at[8], "sib")
    for n in range(3):
        for side in SIDES:
            start(id_copies[side, n])
    forward((0, 0, 0, 128))
    for side in SIDES:
        for n in range(3):
            id_copies[side, n].wait_recv()
        start(id_copies[side, 3])
    id_copies["y", 3].wait_recv()
    for (pair, off), pos in POS.items():
        col_ids[:, pos * 128 : pos * 128 + 128] = idt[pair, off]
    id_copies["x", 3].wait_recv()
    start(id_copies["x", 4])
    receive_slot(0)
    send_slot(2)
    id_copies["x", 4].wait_recv()
    for kind in range(2):
        for (pair, off), pos in POS.items():
            at = pos * 256 + kind * 128
            row_ids[at : at + 128, :] = jnp.broadcast_to(idx[kind, pair, off], (128, 128)).T
    receive_slot(1)
    send_slot(3)
    receive_sibling(0, 1)

    loss_acc[...] = jnp.zeros_like(loss_acc)
    scores = (score0, score1)

    def tile(t):
        k = (t + 15) // 16 + (t + 12) // 16 + (t + 7) // 16
        u = t - k * k
        f = (u - k + 8) // 8
        r = k + f * (u - 2 * k)
        c = u + f * (k - u)
        return pl.multiple_of(r * ROW_TILE, ROW_TILE), pl.multiple_of(c * COL_TILE, COL_TILE)

    def product(t, out):
        r, c = tile(t)
        out[...] = lax.dot_general(
            images[pl.ds(r, ROW_TILE), :],
            texts[pl.ds(c, COL_TILE), :],
            (((1,), (1,)), ((), ())),
            preferred_element_type=F32,
        )

    def pointwise(t, scored):
        r, c = tile(t)
        cols = pl.ds(c, COL_TILE)
        ids = col_ids[:, cols]
        total = jnp.zeros((SLICE, COL_TILE), F32)
        for q in range(ROW_TILE // SLICE):
            rows = pl.ds(r + q * SLICE, SLICE)
            block = row_ids[rows, :]
            positive = jnp.concatenate([block, block], axis=1) == ids
            scale = jnp.where(positive, -sharp, sharp)
            shift = jnp.where(positive, -offset, offset)
            grown = jnp.exp(scale * scored[q * SLICE : (q + 1) * SLICE, :] + shift)
            above = 1.0 + grown
            share = grown * pl.reciprocal(above, approx=True)
            coef[rows, cols] = (share * scale).astype(BF16)
            if q % 8 == 0:
                small = grown
                logs = jnp.log(above)
            else:
                small = small + grown
                logs = logs + jnp.log(above)
            if q % 8 == 7:
                total = total + jnp.where(small < 1e-3, small, logs)
        coef_t[cols, pl.ds(r, ROW_TILE)] = coef[pl.ds(r, ROW_TILE), cols].T
        summed = loss_acc[...]
        for a in range(SLICE // 8):
            for b in range(COL_TILE // 128):
                summed = summed + total[a * 8 : a * 8 + 8, b * 128 : b * 128 + 128]
        loss_acc[...] = summed

    product(0, score0)
    receive_sibling(2, 3)

    def two_tiles(h, _):
        t = 2 * h
        product(t + 1, score1)
        pointwise(t, score0)

        product(t + 2, score0)
        pointwise(t + 1, score1)
        return 0

    two_tiles(0, 0)
    receive_slot(2)
    send_slot(4)
    product(3, score1)
    pointwise(2, score0)
    receive_slot(3)
    receive_sibling(4, 5)
    product(4, score0)
    pointwise(3, score1)
    lax.fori_loop(2, 4, two_tiles, 0)
    receive_slot(4)
    receive_sibling(6, 7)
    lax.fori_loop(4, 7, two_tiles, 0)
    product(15, score1)
    pointwise(14, score0)
    pointwise(15, score1)

    loss_copies = []

    def loss_step():
        n = len(loss_copies)
        if n:
            loss_copies[-1].wait_recv()
            total = loss_send[n - 1] + loss_recv[n - 1]
        else:
            total = loss_acc[...]
        if n < len(LOSS_STEPS):
            loss_send[n] = total
            copy = remote(loss_send.at[n], loss_recv.at[n], l_ss.at[n], l_rs.at[n], LOSS_STEPS[n])
            start(copy)
            loss_copies.append(copy)
        else:
            loss_out[0] = jnp.sum(total) / BATCH

    loss_step()

    parts = {"x": img_part, "y": txt_part}
    returns = {}
    for side in SIDES:
        for event in EVENTS:
            k, link = event
            n = INDEX[event] + (0 if side == "x" else len(EVENTS))
            entry = SENDS[link][k]
            at = n * 64
            returns[side, event] = remote(
                back_send.at[pl.ds(at, 64)], back_recv.at[pl.ds(at, 64)], b_ss.at[n], b_rs.at[n], side + BACK[link]
            )
    sibling = []

    def group(g):
        full = jnp.dot(coef[g * 512 : g * 512 + 512, :], texts[...], preferred_element_type=F32)
        for j in range(2):
            at = (2 * g + j) * 128
            sib_send[at : at + 128, :] = full[j * 256 + 128 : j * 256 + 256].astype(BF16)
            img_part[at : at + 128, :] = full[j * 256 : j * 256 + 128]
        copy = remote(
            sib_send.at[pl.ds(g * 256, 256)], sib_recv.at[pl.ds(g * 256, 256)], p_ss.at[g], p_rs.at[g], "sib"
        )
        start(copy)
        txt_part[g * 256 : g * 256 + 256, :] = jnp.dot(
            coef_t[g * 256 : g * 256 + 256, :], images[...], preferred_element_type=F32
        )
        copy.wait_recv()

    taken = set()

    def total_of(side, pair, off, first, last):
        at = POS[(pair, off)] * 128 + first
        value = parts[side][at : at + last - first, :]
        if side == "x":
            value = value + sib_recv[at : at + last - first, :].astype(F32)
        for event in EVENTS:
            k, link = event
            entry = SENDS[link][k]
            if entry == (pair, off, first, last):
                returns[side, event].wait_recv()
                taken.add((side, event))
                n = INDEX[event] + (0 if side == "x" else len(EVENTS))
                value = value + back_recv[n * 64 : n * 64 + 64, :].astype(F32)
        return value

    def send_back(events):
        for event in events:
            for side in SIDES:
                k, link = event
                n = INDEX[event] + (0 if side == "x" else len(EVENTS))
                value = total_of(side, *landing(link, SENDS[link][k]))
                back_send[n * 64 : n * 64 + 64, :] = value.astype(BF16)
                start(returns[side, event])

    group(3)
    send_back(RETURNS[0])
    loss_step()
    group(2)
    send_back(RETURNS[1])
    loss_step()
    group(1)
    loss_step()
    send_back(RETURNS[2])
    group(0)
    loss_step()
    send_back(RETURNS[3])
    loss_step()
    send_back(RETURNS[4])
    loss_step()
    for half in (0, 64):
        for side, out in (("x", img_out), ("y", txt_out)):
            unit, inverse = normalize(raw[side][half : half + 64, :])
            direction = total_of(side, 0, 0, half, half + 64)
            along = jnp.sum(unit * direction, axis=-1, keepdims=True)
            out[half : half + 64, :] = inverse * (direction - unit * along)
    loss_step()
    for copy in pending:
        copy.wait_send()


def on_device(photo, sentence, photo_ids, sentence_ids, sharp, offset):
    vmem = pl.BlockSpec(memory_space=pltpu.VMEM)
    smem = pl.BlockSpec(memory_space=pltpu.SMEM)
    events = 2 * len(EVENTS)
    dma = pltpu.SemaphoreType.DMA
    return pl.pallas_call(
        kernel,
        out_shape=(
            jax.ShapeDtypeStruct((ROWS, D), F32),
            jax.ShapeDtypeStruct((ROWS, D), F32),
            jax.ShapeDtypeStruct((1,), F32),
        ),
        in_specs=[vmem] * 4 + [smem] * 2,
        out_specs=(vmem, vmem, smem),
        scratch_shapes=[
            pltpu.VMEM((2048, D), BF16),
            pltpu.VMEM((1024, D), BF16),
            pltpu.VMEM((2048, 1024), BF16),
            pltpu.VMEM((1024, 2048), BF16),
            pltpu.VMEM((ROW_TILE, COL_TILE), F32),
            pltpu.VMEM((ROW_TILE, COL_TILE), F32),
            pltpu.VMEM((2048, 128), jnp.int32),
            pltpu.VMEM((1, 1024), jnp.int32),
            pltpu.VMEM((1024, D), F32),
            pltpu.VMEM((1024, D), F32),
            pltpu.VMEM((8, 128), F32),
            pltpu.VMEM((1024, D), BF16),
            pltpu.VMEM((1024, D), BF16),
            pltpu.VMEM((events * 64, D), BF16),
            pltpu.VMEM((events * 64, D), BF16),
            pltpu.VMEM((2, 2, 4, 1, 128), jnp.int32),
            pltpu.VMEM((2, 4, 1, 128), jnp.int32),
            pltpu.VMEM((7, 8, 128), F32),
            pltpu.VMEM((7, 8, 128), F32),
            dma((events,)), dma((events,)),
            dma((16,)), dma((16,)),
            dma((events,)), dma((events,)),
            dma((4,)), dma((4,)),
            dma((9,)), dma((9,)),
            dma((7,)), dma((7,)),
        ],
        compiler_params=pltpu.CompilerParams(
            collective_id=0, has_side_effects=True, vmem_limit_bytes=60 << 20
        ),
        cost_estimate=pl.CostEstimate(flops=3 * 2 * 2048 * 1024 * D, bytes_accessed=1 << 21, transcendentals=3 << 21),
        name="pair_loss",
    )(photo, sentence, photo_ids.reshape(1, ROWS), sentence_ids.reshape(1, ROWS), sharp, offset)


def solution(mesh):
    return jax.shard_map(
        on_device,
        mesh=mesh,
        in_specs=(
            P(("img", "txt"), None),
            P(("txt", "img"), None),
            P(("img", "txt")),
            P(("txt", "img")),
            P(),
            P(),
        ),
        out_specs=(P(("img", "txt"), None), P(("txt", "img"), None), P()),
        check_vma=False,
    )
```

time: 263 us -> 77.2 us (0.29)
  waiting for transfers between devices: 99.8 us -> 0 us
  blocking collectives: 96.9 us -> 0 us
  Pallas kernels: 0 us -> 70.6 us
  matrix products: 33.4 us -> 0 us
  between operations: 16.9 us -> 3.67 us
  other arithmetic: 12.6 us -> 0 us
    pallas_call x0 -> x1, Pallas kernels: none -> 70.6 us  [on_device(): pl.pallas_call(kernel, out_shape=(jax.ShapeDtypeStruct((ROWS, D), F32), j...]
    psum x1 -> x0, blocking collectives: 66 us -> none  [on_device(): summed_loss_value = lax.psum(share, ('img', 'txt'))]
    all_gather x2 -> x0, waiting for transfers between devices: 51.1 us -> none  [the longest x1 51.1 us: on_device(): lax.all_gather(image_send, 'txt', axis=0, tiled=True)]
    reduce_scatter x2 -> x0, waiting for transfers between devices: 48.7 us -> none  [the longest x1 48.6 us: on_device(): lax.psum_scatter(image_acc, 'txt', scatter_dimension=0, tiled=True)]
    dot_general x3 -> x0, matrix products: 33.4 us -> none  [the longest x1 16.3 us: score_block(): lax.dot_general(picture_row_slice, text_rows, (((1,), (1,)), ((), ())), p...]
    all_gather x2 -> x0, blocking collectives: 30.8 us -> none  [the longest x1 17.6 us: on_device(): lax.all_gather(photo_match_ids, 'txt', axis=0, tiled=True)]
    reduce_sum x4 -> x0, other arithmetic: 4.84 us -> none  [the longest x2 2.63 us: backward_norm(): along = jnp.sum(unit_rows * direction, axis=-1, keepdims=True)]
    mul x2 -> x0, other arithmetic: 4.18 us -> none  [backward_norm(): return inverse * (direction - unit_rows * along)]
  transfers between devices with their start and end apart: 4 -> 0, of which waited for: 2 -> 0; matrix products, arithmetic and copies ran while one was open for 6% -> 0% of each run, Pallas kernels for 0% -> 0%
where the time goes in v1:
time: 77.2 us; the launch traced here: 77 us
  Pallas kernels  70.6 us (91%)
  between operations  3.67 us (5%)
  local copies, waits for them, and re-layouts  2.8 us (4%)
    pallas_call x1, Pallas kernels, on_device(): pl.pallas_call(kernel, out_shape=(jax.ShapeDtypeStruct((ROWS, D), F32), j...  70.6 us
    unnamed x4, local copies, waits for them, and re-layouts  2.8 us

profile of v1, /device:TPU:1, one launch (start us, length us, event | category | flops | bytes accessed | tf_op | source)
XLA Modules:
  0.0 77.0 jit_solution(10714396495717763310)
XLA Ops:
  1.9 70.6 %pair_loss.1 = (f32[128,1152]{1,0:T(8,128)}, f32[128,1152]{1,0:T(8,128)}, f32[1]{0:T(128)}) custom-call(bf16[128,1152]{1,0:T(8,128)(2,1)} %img_raw.1, bf16[128,1152]{1,0:T(8,128)(2,1)} %txt_raw.1, s32[1,128]{1,0:T(1,128)} %bitcast.2, s32[1,128]{1,0:T(1,128)} %bitcast.3, f32[1]{0:T(128)S(6)} %copy.12.sharp_ref, f32[1]{0:T(128)S(6)} %copy.13.offset_ref), custom_call_target="tpu_custom_call" | custom-call | flops 14495514624 | bytes 2097152 | tf_op jit(solution)/shard_map/pair_loss/pallas_call | solution.py:377
  72.5 0.0 copy-start
  72.5 2.0 %copy.14 = f32[128,1152]{1,0:T(8,128)} copy(f32[128,1152]{1,0:T(8,128)} %get-tuple-element.6) | data formatting | bytes 1179648
  74.5 0.0 copy-done
  74.5 0.8 %copy.15 = f32[128,1152]{1,0:T(8,128)} copy(f32[128,1152]{1,0:T(8,128)S(1)} %copy-done) | data formatting | bytes 1179648
Async XLA Ops:
  72.5 2.0 %copy-start = (f32[128,1152]{1,0:T(8,128)S(1)}, f32[128,1152]{1,0:T(8,128)}, u32[]{:S(2)}) copy-start(f32[128,1152]{1,0:T(8,128)} %get-tuple-element.7) | copy-start | bytes 1769476

commit v2 on v1

v2 whole, which is shorter than its diff:
```python
import functools

import jax
import jax.numpy as jnp
from jax import lax
from jax.experimental import pallas as pl
from jax.experimental.pallas import tpu as pltpu
from jax.sharding import PartitionSpec as P

MESH = pl.DeviceIdType.MESH
EPSILON = 1e-06
D = 1152
ROWS = 128
BATCH = 16384
F32 = jnp.float32
BF16 = jnp.bfloat16

POS = {(0, 0): 0, (0, 1): 1, (0, 3): 2, (1, 0): 3, (1, 1): 4, (0, 2): 5, (1, 3): 6, (1, 2): 7}
SENDS = {
    "R": [(0, 0, 64, 128), (0, 0, 0, 64), (1, 0, 0, 64), (0, 3, 64, 128), (1, 3, 0, 64)],
    "L": [(0, 0, 64, 128), (0, 0, 0, 64), (1, 0, 0, 64), (0, 1, 0, 64), (1, 1, 64, 128)],
    "V": [(0, 0, 0, 64), (0, 0, 64, 128), (0, 1, 64, 128), (0, 3, 64, 128)],
}
EVENTS = [(k, link) for k in range(5) for link in "RLV" if k < len(SENDS[link])]
INDEX = {event: i for i, event in enumerate(EVENTS)}
BACK = {"R": "L", "L": "R", "V": "V"}
RETURNS = [
    [(4, "R"), (4, "L")],
    [(3, "R"), (3, "L"), (3, "V")],
    [(2, "R"), (2, "L"), (2, "V")],
    [(1, "R"), (1, "L"), (1, "V")],
    [(0, "R"), (0, "L"), (0, "V")],
]
SIDES = "xy"
SLICE = 16


def landing(link, entry):
    pair, offset, first, last = entry
    if link == "R":
        return (pair, (offset + 3) % 4, first, last)
    if link == "L":
        return (pair, (offset + 1) % 4, first, last)
    return (1 - pair, offset, first, last)


def partners():
    i = lax.axis_index("img")
    t = lax.axis_index("txt")
    z, c, y, x = i // 2, i % 2, t // 4, t % 4

    def at(x, y, z, c):
        return (z * 2 + c, y * 4 + x)

    return {
        "xR": at((x + 1) % 4, y, z, c),
        "xL": at((x + 3) % 4, y, z, c),
        "xV": at(x, y, z + 1 - 2 * (z % 2), c),
        "x2": at((x + 2) % 4, y, z, c),
        "xVR": at((x + 1) % 4, y, z + 1 - 2 * (z % 2), c),
        "xVL": at((x + 3) % 4, y, z + 1 - 2 * (z % 2), c),
        "xV2": at((x + 2) % 4, y, z + 1 - 2 * (z % 2), c),
        "yR": at(x, (y + 1) % 4, z, c),
        "yL": at(x, (y + 3) % 4, z, c),
        "yV": at(x, y, 3 - z, c),
        "y2": at(x, (y + 2) % 4, z, c),
        "yVR": at(x, (y + 1) % 4, 3 - z, c),
        "yVL": at(x, (y + 3) % 4, 3 - z, c),
        "yV2": at(x, (y + 2) % 4, 3 - z, c),
        "sib": at(x, y, z, 1 - c),
    }


PLACES = {"R": (0, 3), "L": (0, 1), "2": (0, 2), "V": (1, 0), "VR": (1, 3), "VL": (1, 1), "V2": (1, 2)}
BARRIER = tuple(side + name for side in SIDES for name in PLACES) + ("sib",)
LOSS_STEPS = (("sib",), ("xV",), ("yV",), ("xR", "xL", "x2"), ("yR", "yL", "y2"))


def normalize(values):
    wide = values.astype(F32)
    inverse = lax.rsqrt(jnp.sum(wide * wide, axis=-1, keepdims=True) + EPSILON)
    return wide * inverse, inverse


def kernel(
    img_hbm, txt_hbm, img_ids, txt_ids, sharp_ref, offset_ref,
    img_out, txt_out, loss_out,
    images, texts, coef, coef_t, score0, score1, img_rows, img_lanes, txt_rows, txt_lanes, img_part, txt_part, loss_acc,
    sib_send, sib_recv, back_send, back_recv, idx, idt, loss_held,
    img_raw, txt_raw, in_sem, g_ss, g_rs, f_ss, f_rs, b_ss, b_rs, p_ss, p_rs, i_ss, i_rs, l_ss, l_rs,
):
    to = partners()
    sharp = sharp_ref[0]
    offset = offset_ref[0]
    raw = {"x": img_raw, "y": txt_raw}

    def remote(src, dst, send, recv, where):
        return pltpu.make_async_remote_copy(
            src_ref=src, dst_ref=dst, send_sem=send, recv_sem=recv, device_id=to[where], device_id_type=MESH
        )

    pending = []

    def start(copy):
        copy.start()
        pending.append(copy)

    barrier = pltpu.get_barrier_semaphore()
    for name in BARRIER:
        pl.semaphore_signal(barrier, inc=1, device_id=to[name], device_id_type=MESH)
    img_load = pltpu.make_async_copy(img_hbm, img_raw, in_sem.at[0])
    txt_load = pltpu.make_async_copy(txt_hbm, txt_raw, in_sem.at[1])
    img_load.start()
    txt_load.start()
    img_load.wait()
    images[0:ROWS, :] = normalize(img_raw[...])[0].astype(BF16)
    txt_load.wait()
    texts[0:ROWS, :] = normalize(txt_raw[...])[0].astype(BF16)
    idx[0, 0, 0] = img_ids[...]
    idt[0, 0] = txt_ids[...]
    pl.semaphore_wait(barrier, len(BARRIER))

    def rows_of(side, entry):
        pair, off, first, last = entry
        pos = POS[(pair, off)]
        if side == "x":
            return images.at[pl.ds(pos * 256 + first, last - first)]
        return texts.at[pl.ds(pos * 128 + first, last - first)]

    gather = {}
    for side in SIDES:
        for event in EVENTS:
            k, link = event
            n = INDEX[event] + (0 if side == "x" else len(EVENTS))
            entry = SENDS[link][k]
            gather[side, event] = remote(
                rows_of(side, entry), rows_of(side, landing(link, entry)), g_ss.at[n], g_rs.at[n], side + link
            )

    forwards = {}

    def forward(entry):
        n = sum(len(copies) for copies in forwards.values())
        pair, off, first, last = entry
        at = POS[(pair, off)] * 256 + first
        copy = remote(
            images.at[pl.ds(at, last - first)], images.at[pl.ds(at + 128, last - first)], f_ss.at[n], f_rs.at[n], "sib"
        )
        start(copy)
        forwards.setdefault(POS[(pair, off)], []).append(copy)

    def send_slot(k):
        for event in EVENTS:
            if event[0] == k:
                for side in SIDES:
                    start(gather[side, event])

    def receive_slot(k):
        for event in EVENTS:
            if event[0] == k:
                for side in SIDES:
                    gather[side, event].wait_recv()
                forward(landing(event[1], SENDS[event[1]][k]))

    def receive_sibling(*positions):
        for pos in positions:
            for copy in forwards[pos]:
                copy.wait_recv()

    id_copies = []
    for name, place in PLACES.items():
        for side, ids in (("x", idx.at[0]), ("y", idt)):
            n = len(id_copies)
            id_copies.append(remote(ids.at[0, 0], ids.at[place], i_ss.at[n], i_rs.at[n], side + name))
            start(id_copies[n])
    send_slot(0)
    send_slot(1)
    forward((0, 0, 0, 128))
    for copy in id_copies:
        copy.wait_recv()
    id_forward = remote(idx.at[0], idx.at[1], i_ss.at[14], i_rs.at[14], "sib")
    start(id_forward)
    for (pair, off), pos in POS.items():
        txt_lanes[:, pos * 128 : pos * 128 + 128] = idt[pair, off]
        if pos == 7:
            txt_rows[...] = jnp.broadcast_to(idt[pair, off], (128, 128)).T

    def spread(kind):
        for (pair, off), pos in POS.items():
            at = pos * 256 + kind * 128
            img_lanes[:, at : at + 128] = idx[kind, pair, off]
            img_rows[at : at + 128, :] = jnp.broadcast_to(idx[kind, pair, off], (128, 128)).T

    receive_slot(0)
    send_slot(2)
    spread(0)
    id_forward.wait_recv()
    spread(1)
    receive_slot(1)
    send_slot(3)
    receive_sibling(0, 1)

    sums = []

    def image_group(first, last):
        n = len(sums)
        full = jnp.dot(coef[first * 256 : last * 256, :], texts[...], preferred_element_type=F32)
        for j in range(last - first):
            at = (first + j) * 128
            sib_send[at : at + 128, :] = full[j * 256 + 128 : j * 256 + 256].astype(BF16)
            img_part[at : at + 128, :] = full[j * 256 : j * 256 + 128]
        rows = pl.ds(first * 128, (last - first) * 128)
        sums.append(remote(sib_send.at[rows], sib_recv.at[rows], p_ss.at[n], p_rs.at[n], "sib"))
        start(sums[n])

    def text_group(first, last):
        txt_part[first * 128 : last * 128, :] = jnp.dot(
            coef_t[first * 128 : last * 128, :], images[...], preferred_element_type=F32
        )

    loss_acc[...] = jnp.zeros_like(loss_acc)

    def product(tile, out):
        texts_first, row, height, col, width = tile
        left, right = (texts, images) if texts_first else (images, texts)
        out[0:height, 0:width] = lax.dot_general(
            left[row : row + height, :],
            right[col : col + width, :],
            (((1,), (1,)), ((), ())),
            preferred_element_type=F32,
        )

    def pointwise(tile, scored):
        texts_first, row, height, col, width = tile
        if texts_first:
            out, out_t, lanes, row_ids = coef_t, coef, img_lanes, txt_rows
            row_ids_at = 0
        else:
            out, out_t, lanes, row_ids = coef, coef_t, txt_lanes, img_rows
            row_ids_at = row
        summed = loss_acc[...]
        for left in range(0, width, 512):
            wide = min(512, width - left)
            cols = slice(col + left, col + left + wide)
            ids = lanes[:, cols]
            for q in range(height // SLICE):
                block = row_ids[row_ids_at + q * SLICE : row_ids_at + (q + 1) * SLICE, :]
                positive = jnp.concatenate([block] * (wide // 128), axis=1) == ids
                scale = jnp.where(positive, -sharp, sharp)
                shift = jnp.where(positive, -offset, offset)
                grown = jnp.exp(scale * scored[q * SLICE : (q + 1) * SLICE, left : left + wide] + shift)
                above = 1.0 + grown
                share = grown * pl.reciprocal(above, approx=True)
                out[row + q * SLICE : row + (q + 1) * SLICE, cols] = (share * scale).astype(BF16)
                if q % 8 == 0:
                    small = grown
                    logs = jnp.log(above)
                else:
                    small = small + grown
                    logs = logs + jnp.log(above)
                if q == 7:
                    total = jnp.where(small < 1e-3, small, logs)
                elif q % 8 == 7:
                    total = total + jnp.where(small < 1e-3, small, logs)
            for a in range(0, SLICE, 8):
                for b in range(0, wide, 128):
                    summed = summed + total[a : a + 8, b : b + 128]
        loss_acc[...] = summed
        rows = slice(row, row + height)
        cols = slice(col, col + width)
        out_t[cols, rows] = out[rows, cols].T

    scores = (score0, score1)
    done = []

    def score(*tiles):
        for tile in tiles:
            product(tile, scores[len(done) % 2])
            if done:
                pointwise(done[-1], scores[(len(done) - 1) % 2])
            done.append(tile)

    score((False, 0, 256, 0, 512), (False, 256, 256, 0, 512))
    receive_sibling(2, 3)
    score((False, 512, 256, 0, 512))
    receive_slot(2)
    send_slot(4)
    score((False, 768, 256, 0, 512))
    receive_sibling(4)
    score((False, 1024, 256, 0, 512))
    receive_slot(3)
    score(*((False, at, 256, 512, 384) for at in range(0, 1280, 256)))
    receive_sibling(5, 6)
    for at in (1280, 1536):
        score((False, at, 256, 0, 512), (False, at, 256, 512, 384))
    receive_slot(4)
    score((True, 896, 128, 0, 896), (True, 896, 128, 896, 896))
    receive_sibling(7)
    score((False, 1792, 256, 0, 512), (False, 1792, 256, 512, 512))
    pointwise(done[-1], scores[(len(done) - 1) % 2])
    image_group(7, 8)

    place = {"x": lax.axis_index("txt") % 4, "y": lax.axis_index("txt") // 4}
    loss_copies = []

    def loss_step():
        n = len(loss_copies)
        if n:
            for copy in loss_copies[-1]:
                copy.wait_recv()
            before = LOSS_STEPS[n - 1]
            if len(before) == 1:
                total = loss_held[n - 1, 0] + loss_held[n - 1, 1]
            else:
                total = (loss_held[n - 1, 0] + loss_held[n - 1, 1]) + (loss_held[n - 1, 2] + loss_held[n - 1, 3])
        else:
            total = loss_acc[...]
        if n < len(LOSS_STEPS):
            where = LOSS_STEPS[n]
            mine, theirs = (0, 1) if len(where) == 1 else (place[where[0][0]],) * 2
            loss_held[n, mine] = total
            copies = []
            for j, name in enumerate(where):
                copy = remote(
                    loss_held.at[n, mine], loss_held.at[n, theirs], l_ss.at[n, j], l_rs.at[n, j], name
                )
                start(copy)
                copies.append(copy)
            loss_copies.append(copies)
        else:
            loss_out[0] = jnp.sum(total) / BATCH

    loss_step()

    parts = {"x": img_part, "y": txt_part}
    returns = {}
    for side in SIDES:
        for event in EVENTS:
            k, link = event
            n = INDEX[event] + (0 if side == "x" else len(EVENTS))
            entry = SENDS[link][k]
            at = n * 64
            returns[side, event] = remote(
                back_send.at[pl.ds(at, 64)], back_recv.at[pl.ds(at, 64)], b_ss.at[n], b_rs.at[n], side + BACK[link]
            )
    sibling = []

    def total_of(side, pair, off, first, last):
        at = POS[(pair, off)] * 128 + first
        value = parts[side][at : at + last - first, :]
        if side == "x":
            value = value + sib_recv[at : at + last - first, :].astype(F32)
        for event in EVENTS:
            k, link = event
            entry = SENDS[link][k]
            if entry == (pair, off, first, last):
                returns[side, event].wait_recv()
                n = INDEX[event] + (0 if side == "x" else len(EVENTS))
                value = value + back_recv[n * 64 : n * 64 + 64, :].astype(F32)
        return value

    def send_back(slot, sides):
        for event in RETURNS[slot]:
            for side in sides:
                k, link = event
                n = INDEX[event] + (0 if side == "x" else len(EVENTS))
                value = total_of(side, *landing(link, SENDS[link][k]))
                back_send[n * 64 : n * 64 + 64, :] = value.astype(BF16)
                start(returns[side, event])

    text_group(7, 8)
    send_back(0, "y")
    loss_step()
    sums[0].wait_recv()
    send_back(0, "x")
    image_group(5, 7)
    text_group(5, 7)
    send_back(1, "y")
    loss_step()
    sums[1].wait_recv()
    send_back(1, "x")
    image_group(4, 5)
    text_group(4, 5)
    send_back(2, "y")
    loss_step()
    sums[2].wait_recv()
    send_back(2, "x")
    image_group(1, 4)
    text_group(1, 4)
    send_back(3, "y")
    loss_step()
    sums[3].wait_recv()
    send_back(3, "x")
    send_back(4, "yx")
    image_group(0, 1)
    text_group(0, 1)
    sums[4].wait_recv()
    for half in (0, 64):
        for side, out in (("x", img_out), ("y", txt_out)):
            unit, inverse = normalize(raw[side][half : half + 64, :])
            direction = total_of(side, 0, 0, half, half + 64)
            along = jnp.sum(unit * direction, axis=-1, keepdims=True)
            out[half : half + 64, :] = inverse * (direction - unit * along)
    loss_step()
    for copy in pending:
        copy.wait_send()


def on_device(photo, sentence, photo_ids, sentence_ids, sharp, offset):
    vmem = pl.BlockSpec(memory_space=pltpu.VMEM)
    smem = pl.BlockSpec(memory_space=pltpu.SMEM)
    events = 2 * len(EVENTS)
    dma = pltpu.SemaphoreType.DMA
    return pl.pallas_call(
        kernel,
        out_shape=(
            pltpu.VMEM((ROWS, D), F32),
            pltpu.VMEM((ROWS, D), F32),
            jax.ShapeDtypeStruct((1,), F32),
        ),
        in_specs=[pl.BlockSpec(memory_space=pl.ANY)] * 2 + [vmem] * 2 + [smem] * 2,
        out_specs=(vmem, vmem, smem),
        scratch_shapes=[
            pltpu.VMEM((2048, D), BF16),
            pltpu.VMEM((1024, D), BF16),
            pltpu.VMEM((2048, 1024), BF16),
            pltpu.VMEM((1024, 2048), BF16),
            pltpu.VMEM((256, 896), F32),
            pltpu.VMEM((256, 896), F32),
            pltpu.VMEM((2048, 128), jnp.int32),
            pltpu.VMEM((1, 2048), jnp.int32),
            pltpu.VMEM((128, 128), jnp.int32),
            pltpu.VMEM((1, 1024), jnp.int32),
            pltpu.VMEM((1024, D), F32),
            pltpu.VMEM((1024, D), F32),
            pltpu.VMEM((8, 128), F32),
            pltpu.VMEM((1024, D), BF16),
            pltpu.VMEM((1024, D), BF16),
            pltpu.VMEM((events * 64, D), BF16),
            pltpu.VMEM((events * 64, D), BF16),
            pltpu.VMEM((2, 2, 4, 1, 128), jnp.int32),
            pltpu.VMEM((2, 4, 1, 128), jnp.int32),
            pltpu.VMEM((5, 4, 8, 128), F32),
            pltpu.VMEM((ROWS, D), BF16),
            pltpu.VMEM((ROWS, D), BF16),
            dma((2,)),
            dma((events,)), dma((events,)),
            dma((16,)), dma((16,)),
            dma((events,)), dma((events,)),
            dma((5,)), dma((5,)),
            dma((15,)), dma((15,)),
            dma((5, 3)), dma((5, 3)),
        ],
        compiler_params=pltpu.CompilerParams(
            collective_id=0, has_side_effects=True, vmem_limit_bytes=60 << 20
        ),
        cost_estimate=pl.CostEstimate(flops=3 * 2 * 2048 * 1024 * D, bytes_accessed=1 << 21, transcendentals=3 << 21),
        name="pair_loss",
    )(photo, sentence, photo_ids.reshape(1, ROWS), sentence_ids.reshape(1, ROWS), sharp, offset)


def solution(mesh):
    return jax.shard_map(
        on_device,
        mesh=mesh,
        in_specs=(
            P(("img", "txt"), None),
            P(("txt", "img"), None),
            P(("img", "txt")),
            P(("txt", "img")),
            P(),
            P(),
        ),
        out_specs=(P(("img", "txt"), None), P(("txt", "img"), None), P()),
        check_vma=False,
    )
```

time: 77.2 us -> 65.4 us (0.85)
  Pallas kernels: 70.6 us -> 60 us
  local copies, waits for them, and re-layouts: 2.8 us -> 1.63 us
    pallas_call x1, Pallas kernels: 70.6 us -> 60 us  [on_device(): pl.pallas_call(kernel, out_shape=(pltpu.VMEM((ROWS, D), F32), pltpu.VMEM(...]
    unnamed x4 -> x2, local copies, waits for them, and re-layouts: 2.8 us -> 1.63 us
where the time goes in v2:
time: 65.4 us; the launch traced here: 65.2 us
  Pallas kernels  60 us (92%)
  between operations  3.62 us (6%)
  local copies, waits for them, and re-layouts  1.63 us (2%)
    pallas_call x1, Pallas kernels, on_device(): pl.pallas_call(kernel, out_shape=(pltpu.VMEM((ROWS, D), F32), pltpu.VMEM(...  60 us
    unnamed x2, local copies, waits for them, and re-layouts  1.63 us

profile of v2, /device:TPU:1, one launch (start us, length us, event | category | flops | bytes accessed | tf_op | source)
XLA Modules:
  0.0 65.2 jit_solution(16440344600260818303)
XLA Ops:
  1.9 60.0 %pair_loss.1 = (f32[128,1152]{1,0:T(8,128)S(1)}, f32[128,1152]{1,0:T(8,128)S(1)}, f32[1]{0:T(128)}) custom-call(bf16[128,1152]{1,0:T(8,128)(2,1)} %img_hbm.1, bf16[128,1152]{1,0:T(8,128)(2,1)} %txt_hbm.1, s32[1,128]{1,0:T(1,128)} %bitcast.2, s32[1,128]{1,0:T(1,128)} %bitcast.3, f32[1]{0:T(128)S(6)} %copy.14.sharp_ref, f32[1]{0:T(128)S(6)} %copy.15.offset_ref), custom_call_target="tpu_custom_call" | custom-call | flops 14495514624 | bytes 2097152 | tf_op jit(solution)/shard_map/pair_loss/pallas_call | solution.py:414
  61.9 0.8 %copy.12 = f32[128,1152]{1,0:T(8,128)} copy(f32[128,1152]{1,0:T(8,128)S(1)} %get-tuple-element.3) | data formatting | bytes 1179648
  62.7 0.8 %copy.13 = f32[128,1152]{1,0:T(8,128)} copy(f32[128,1152]{1,0:T(8,128)S(1)} %get-tuple-element.4) | data formatting | bytes 1179648

commit v3 on v2

--- a/solution.py
+++ b/solution.py
@@ -32,7 +32,6 @@
     [(0, "R"), (0, "L"), (0, "V")],
 ]
 SIDES = "xy"
-SLICE = 16
 
 
 def landing(link, entry):
@@ -42,6 +41,17 @@
     if link == "L":
         return (pair, (offset + 1) % 4, first, last)
     return (1 - pair, offset, first, last)
+
+
+ENTRIES = {SENDS[link][k] for k, link in EVENTS}
+LEAVES = {
+    POS[place[:2]] * 128 + place[2]: (k, link)
+    for k, link in EVENTS
+    for place in [landing(link, SENDS[link][k])]
+    if place not in ENTRIES
+}
+SLICE = 16
+TURNED = {4: 0, 7: 128}
 
 
 def partners():
@@ -124,7 +134,7 @@
         pair, off, first, last = entry
         pos = POS[(pair, off)]
         if side == "x":
-            return images.at[pl.ds(pos * 256 + first, last - first)]
+            return images.at[pl.ds(pos * 128 + first, last - first)]
         return texts.at[pl.ds(pos * 128 + first, last - first)]
 
     gather = {}
@@ -142,9 +152,9 @@
     def forward(entry):
         n = sum(len(copies) for copies in forwards.values())
         pair, off, first, last = entry
-        at = POS[(pair, off)] * 256 + first
+        at = POS[(pair, off)] * 128 + first
         copy = remote(
-            images.at[pl.ds(at, last - first)], images.at[pl.ds(at + 128, last - first)], f_ss.at[n], f_rs.at[n], "sib"
+            images.at[pl.ds(at, last - first)], images.at[pl.ds(at + 1024, last - first)], f_ss.at[n], f_rs.at[n], "sib"
         )
         start(copy)
         forwards.setdefault(POS[(pair, off)], []).append(copy)
@@ -182,12 +192,13 @@
     start(id_forward)
     for (pair, off), pos in POS.items():
         txt_lanes[:, pos * 128 : pos * 128 + 128] = idt[pair, off]
-        if pos == 7:
-            txt_rows[...] = jnp.broadcast_to(idt[pair, off], (128, 128)).T
+        if pos in TURNED:
+            at = TURNED[pos]
+            txt_rows[at : at + 128, :] = jnp.broadcast_to(idt[pair, off], (128, 128)).T
 
     def spread(kind):
         for (pair, off), pos in POS.items():
-            at = pos * 256 + kind * 128
+            at = kind * 1024 + pos * 128
             img_lanes[:, at : at + 128] = idx[kind, pair, off]
             img_rows[at : at + 128, :] = jnp.broadcast_to(idx[kind, pair, off], (128, 128)).T
 
@@ -198,25 +209,31 @@
     spread(1)
     receive_slot(1)
     send_slot(3)
-    receive_sibling(0, 1)
 
     sums = []
 
     def image_group(first, last):
         n = len(sums)
-        full = jnp.dot(coef[first * 256 : last * 256, :], texts[...], preferred_element_type=F32)
-        for j in range(last - first):
-            at = (first + j) * 128
-            sib_send[at : at + 128, :] = full[j * 256 + 128 : j * 256 + 256].astype(BF16)
-            img_part[at : at + 128, :] = full[j * 256 : j * 256 + 128]
+        size = (last - first) * 128
+        own = slice(first * 128, last * 128)
+        other = slice(1024 + first * 128, 1024 + last * 128)
+        both = jnp.concatenate([coef[own, :], coef[other, :]], axis=0)
+        full = jnp.dot(both, texts[...], preferred_element_type=F32)
+        img_part[own, :] = full[:size]
+        sib_send[own, :] = full[size:].astype(BF16)
         rows = pl.ds(first * 128, (last - first) * 128)
         sums.append(remote(sib_send.at[rows], sib_recv.at[rows], p_ss.at[n], p_rs.at[n], "sib"))
-        start(sums[n])
 
     def text_group(first, last):
-        txt_part[first * 128 : last * 128, :] = jnp.dot(
-            coef_t[first * 128 : last * 128, :], images[...], preferred_element_type=F32
-        )
+        rows = slice(first * 128, last * 128)
+        full = jnp.dot(coef_t[rows, :], images[...], preferred_element_type=F32)
+        for half in range(first * 128, last * 128, 64):
+            value = full[half - first * 128 : half - first * 128 + 64]
+            if half in LEAVES:
+                n = INDEX[LEAVES[half]] + len(EVENTS)
+                back_send[n * 64 : n * 64 + 64, :] = value.astype(BF16)
+            else:
+                txt_part[half : half + 64, :] = value
 
     loss_acc[...] = jnp.zeros_like(loss_acc)
 
@@ -234,7 +251,7 @@
         texts_first, row, height, col, width = tile
         if texts_first:
             out, out_t, lanes, row_ids = coef_t, coef, img_lanes, txt_rows
-            row_ids_at = 0
+            row_ids_at = TURNED[row // 128]
         else:
             out, out_t, lanes, row_ids = coef, coef_t, txt_lanes, img_rows
             row_ids_at = row
@@ -280,25 +297,26 @@
                 pointwise(done[-1], scores[(len(done) - 1) % 2])
             done.append(tile)
 
-    score((False, 0, 256, 0, 512), (False, 256, 256, 0, 512))
-    receive_sibling(2, 3)
-    score((False, 512, 256, 0, 512))
+    score((False, 0, 512, 0, 512))
+    receive_sibling(0, 1, 2, 3)
+    score((False, 1024, 512, 0, 512))
     receive_slot(2)
     send_slot(4)
-    score((False, 768, 256, 0, 512))
+    score((False, 512, 128, 0, 512), (True, 512, 128, 0, 640))
     receive_sibling(4)
-    score((False, 1024, 256, 0, 512))
+    score((False, 1536, 128, 0, 512), (True, 512, 128, 1024, 640))
     receive_slot(3)
-    score(*((False, at, 256, 512, 384) for at in range(0, 1280, 256)))
+    score((False, 0, 640, 640, 256), (False, 1024, 640, 640, 256))
+    score((False, 640, 256, 0, 512), (False, 640, 256, 512, 384))
     receive_sibling(5, 6)
-    for at in (1280, 1536):
-        score((False, at, 256, 0, 512), (False, at, 256, 512, 384))
     receive_slot(4)
-    score((True, 896, 128, 0, 896), (True, 896, 128, 896, 896))
+    score((False, 1664, 256, 0, 512), (False, 1664, 256, 512, 384))
+    score((False, 896, 128, 0, 1024), (True, 896, 128, 0, 896))
     receive_sibling(7)
-    score((False, 1792, 256, 0, 512), (False, 1792, 256, 512, 512))
+    score((False, 1920, 128, 0, 1024), (True, 896, 128, 1024, 896))
+    image_group(7, 8)
+    start(sums[0])
     pointwise(done[-1], scores[(len(done) - 1) % 2])
-    image_group(7, 8)
 
     place = {"x": lax.axis_index("txt") % 4, "y": lax.axis_index("txt") // 4}
     loss_copies = []
@@ -364,35 +382,40 @@
             for side in sides:
                 k, link = event
                 n = INDEX[event] + (0 if side == "x" else len(EVENTS))
-                value = total_of(side, *landing(link, SENDS[link][k]))
-                back_send[n * 64 : n * 64 + 64, :] = value.astype(BF16)
+                if side == "x" or event not in LEAVES.values():
+                    value = total_of(side, *landing(link, SENDS[link][k]))
+                    back_send[n * 64 : n * 64 + 64, :] = value.astype(BF16)
                 start(returns[side, event])
 
     text_group(7, 8)
+    image_group(5, 7)
+    start(sums[1])
+    loss_step()
     send_back(0, "y")
-    loss_step()
     sums[0].wait_recv()
     send_back(0, "x")
-    image_group(5, 7)
     text_group(5, 7)
+    image_group(4, 5)
+    start(sums[2])
+    loss_step()
     send_back(1, "y")
-    loss_step()
     sums[1].wait_recv()
     send_back(1, "x")
-    image_group(4, 5)
     text_group(4, 5)
+    image_group(1, 4)
+    start(sums[3])
+    loss_step()
     send_back(2, "y")
-    loss_step()
     sums[2].wait_recv()
     send_back(2, "x")
-    image_group(1, 4)
     text_group(1, 4)
+    loss_step()
     send_back(3, "y")
-    loss_step()
     sums[3].wait_recv()
     send_back(3, "x")
     send_back(4, "yx")
     image_group(0, 1)
+    start(sums[4])
     text_group(0, 1)
     sums[4].wait_recv()
     for half in (0, 64):
@@ -425,11 +448,11 @@
             pltpu.VMEM((1024, D), BF16),
             pltpu.VMEM((2048, 1024), BF16),
             pltpu.VMEM((1024, 2048), BF16),
-            pltpu.VMEM((256, 896), F32),
-            pltpu.VMEM((256, 896), F32),
+            pltpu.VMEM((640, 1024), F32),
+            pltpu.VMEM((640, 1024), F32),
             pltpu.VMEM((2048, 128), jnp.int32),
             pltpu.VMEM((1, 2048), jnp.int32),
-            pltpu.VMEM((128, 128), jnp.int32),
+            pltpu.VMEM((256, 128), jnp.int32),
             pltpu.VMEM((1, 1024), jnp.int32),
             pltpu.VMEM((1024, D), F32),
             pltpu.VMEM((1024, D), F32),

time: 65.4 us -> 62 us (0.948)
  Pallas kernels: 60 us -> 56.6 us
    pallas_call x1, Pallas kernels: 60 us -> 56.6 us  [on_device(): pl.pallas_call(kernel, out_shape=(pltpu.VMEM((ROWS, D), F32), pltpu.VMEM(...]
where the time goes in v3:
time: 62 us; the launch traced here: 61.9 us
  Pallas kernels  56.6 us (91%)
  between operations  3.62 us (6%)
  local copies, waits for them, and re-layouts  1.63 us (3%)
    pallas_call x1, Pallas kernels, on_device(): pl.pallas_call(kernel, out_shape=(pltpu.VMEM((ROWS, D), F32), pltpu.VMEM(...  56.6 us
    unnamed x2, local copies, waits for them, and re-layouts  1.63 us

profile of v3, /device:TPU:1, one launch (start us, length us, event | category | flops | bytes accessed | tf_op | source)
XLA Modules:
  0.0 61.9 jit_solution(7484784891043693076)
XLA Ops:
  1.9 56.6 %pair_loss.1 = (f32[128,1152]{1,0:T(8,128)S(1)}, f32[128,1152]{1,0:T(8,128)S(1)}, f32[1]{0:T(128)}) custom-call(bf16[128,1152]{1,0:T(8,128)(2,1)} %img_hbm.1, bf16[128,1152]{1,0:T(8,128)(2,1)} %txt_hbm.1, s32[1,128]{1,0:T(1,128)} %bitcast.2, s32[1,128]{1,0:T(1,128)} %bitcast.3, f32[1]{0:T(128)S(6)} %copy.14.sharp_ref, f32[1]{0:T(128)S(6)} %copy.15.offset_ref), custom_call_target="tpu_custom_call" | custom-call | flops 14495514624 | bytes 2097152 | tf_op jit(solution)/shard_map/pair_loss/pallas_call | solution.py:437
  58.6 0.8 %copy.12 = f32[128,1152]{1,0:T(8,128)} copy(f32[128,1152]{1,0:T(8,128)S(1)} %get-tuple-element.3) | data formatting | bytes 1179648
  59.4 0.8 %copy.13 = f32[128,1152]{1,0:T(8,128)} copy(f32[128,1152]{1,0:T(8,128)S(1)} %get-tuple-element.4) | data formatting | bytes 1179648

commit v4 on v3

--- a/solution.py
+++ b/solution.py
@@ -78,12 +78,16 @@
         "yVL": at(x, (y + 3) % 4, 3 - z, c),
         "yV2": at(x, (y + 2) % 4, 3 - z, c),
         "sib": at(x, y, z, 1 - c),
+        "z2": at(x, y, (z + 2) % 4, c),
+        "z1s": at(x, y, z + 1 - 2 * (z % 2), 1 - c),
+        "z2s": at(x, y, (z + 2) % 4, 1 - c),
+        "z3s": at(x, y, 3 - z, 1 - c),
     }
 
 
 PLACES = {"R": (0, 3), "L": (0, 1), "2": (0, 2), "V": (1, 0), "VR": (1, 3), "VL": (1, 1), "V2": (1, 2)}
-BARRIER = tuple(side + name for side in SIDES for name in PLACES) + ("sib",)
-LOSS_STEPS = (("sib",), ("xV",), ("yV",), ("xR", "xL", "x2"), ("yR", "yL", "y2"))
+BARRIER = tuple(side + name for side in SIDES for name in PLACES) + ("sib", "z2", "z1s", "z2s", "z3s")
+LOSS_STEPS = (("xR", "xL", "x2"), ("yR", "yL", "y2"), ("xV", "yV", "z2", "sib", "z1s", "z2s", "z3s"))
 
 
 def normalize(values):
@@ -97,7 +101,7 @@
     img_out, txt_out, loss_out,
     images, texts, coef, coef_t, score0, score1, img_rows, img_lanes, txt_rows, txt_lanes, img_part, txt_part, loss_acc,
     sib_send, sib_recv, back_send, back_recv, idx, idt, loss_held,
-    img_raw, txt_raw, in_sem, g_ss, g_rs, f_ss, f_rs, b_ss, b_rs, p_ss, p_rs, i_ss, i_rs, l_ss, l_rs,
+    img_unit, img_inverse, txt_unit, txt_inverse, img_raw, txt_raw, in_sem, g_ss, g_rs, f_ss, f_rs, b_ss, b_rs, p_ss, p_rs, i_ss, i_rs, l_ss, l_rs,
 ):
     to = partners()
     sharp = sharp_ref[0]
@@ -186,6 +190,8 @@
     send_slot(0)
     send_slot(1)
     forward((0, 0, 0, 128))
+    for side, unit_ref, inverse_ref in (("x", img_unit, img_inverse), ("y", txt_unit, txt_inverse)):
+        unit_ref[...], inverse_ref[...] = normalize(raw[side][...])
     for copy in id_copies:
         copy.wait_recv()
     id_forward = remote(idx.at[0], idx.at[1], i_ss.at[14], i_rs.at[14], "sib")
@@ -315,10 +321,10 @@
     receive_sibling(7)
     score((False, 1920, 128, 0, 1024), (True, 896, 128, 1024, 896))
     image_group(7, 8)
+    pointwise(done[-1], scores[(len(done) - 1) % 2])
     start(sums[0])
-    pointwise(done[-1], scores[(len(done) - 1) % 2])
-
-    place = {"x": lax.axis_index("txt") % 4, "y": lax.axis_index("txt") // 4}
+
+    places = (lax.axis_index("txt") % 4, lax.axis_index("txt") // 4, lax.axis_index("img"))
     loss_copies = []
 
     def loss_step():
@@ -326,29 +332,22 @@
         if n:
             for copy in loss_copies[-1]:
                 copy.wait_recv()
-            before = LOSS_STEPS[n - 1]
-            if len(before) == 1:
-                total = loss_held[n - 1, 0] + loss_held[n - 1, 1]
-            else:
-                total = (loss_held[n - 1, 0] + loss_held[n - 1, 1]) + (loss_held[n - 1, 2] + loss_held[n - 1, 3])
+            total = loss_held[n - 1, 0]
+            for j in range(len(LOSS_STEPS[n - 1])):
+                total = total + loss_held[n - 1, j + 1]
         else:
             total = loss_acc[...]
         if n < len(LOSS_STEPS):
-            where = LOSS_STEPS[n]
-            mine, theirs = (0, 1) if len(where) == 1 else (place[where[0][0]],) * 2
-            loss_held[n, mine] = total
+            loss_held[n, places[n]] = total
             copies = []
-            for j, name in enumerate(where):
-                copy = remote(
-                    loss_held.at[n, mine], loss_held.at[n, theirs], l_ss.at[n, j], l_rs.at[n, j], name
-                )
+            for j, name in enumerate(LOSS_STEPS[n]):
+                mine = loss_held.at[n, places[n]]
+                copy = remote(mine, mine, l_ss.at[n, j], l_rs.at[n, j], name)
                 start(copy)
                 copies.append(copy)
             loss_copies.append(copies)
         else:
             loss_out[0] = jnp.sum(total) / BATCH
-
-    loss_step()
 
     parts = {"x": img_part, "y": txt_part}
     returns = {}
@@ -364,17 +363,16 @@
     sibling = []
 
     def total_of(side, pair, off, first, last):
+        added = [event for event in EVENTS if SENDS[event[1]][event[0]] == (pair, off, first, last)]
+        for event in added:
+            returns[side, event].wait_recv()
         at = POS[(pair, off)] * 128 + first
         value = parts[side][at : at + last - first, :]
         if side == "x":
             value = value + sib_recv[at : at + last - first, :].astype(F32)
-        for event in EVENTS:
-            k, link = event
-            entry = SENDS[link][k]
-            if entry == (pair, off, first, last):
-                returns[side, event].wait_recv()
-                n = INDEX[event] + (0 if side == "x" else len(EVENTS))
-                value = value + back_recv[n * 64 : n * 64 + 64, :].astype(F32)
+        for event in added:
+            n = INDEX[event] + (0 if side == "x" else len(EVENTS))
+            value = value + back_recv[n * 64 : n * 64 + 64, :].astype(F32)
         return value
 
     def send_back(slot, sides):
@@ -397,7 +395,6 @@
     text_group(5, 7)
     image_group(4, 5)
     start(sums[2])
-    loss_step()
     send_back(1, "y")
     sums[1].wait_recv()
     send_back(1, "x")
@@ -418,15 +415,16 @@
     start(sums[4])
     text_group(0, 1)
     sums[4].wait_recv()
-    for half in (0, 64):
-        for side, out in (("x", img_out), ("y", txt_out)):
-            unit, inverse = normalize(raw[side][half : half + 64, :])
-            direction = total_of(side, 0, 0, half, half + 64)
-            along = jnp.sum(unit * direction, axis=-1, keepdims=True)
-            out[half : half + 64, :] = inverse * (direction - unit * along)
-    loss_step()
     for copy in pending:
         copy.wait_send()
+    loss_step()
+    ends = (("x", img_out, img_unit, img_inverse), ("y", txt_out, txt_unit, txt_inverse))
+    for half in (0, 64):
+        for side, out, unit_ref, inverse_ref in ends:
+            direction = total_of(side, 0, 0, half, half + 64)
+            unit = unit_ref[half : half + 64, :]
+            along = jnp.sum(unit * direction, axis=-1, keepdims=True)
+            out[half : half + 64, :] = inverse_ref[half : half + 64, :] * (direction - unit * along)
 
 
 def on_device(photo, sentence, photo_ids, sentence_ids, sharp, offset):
@@ -463,7 +461,11 @@
             pltpu.VMEM((events * 64, D), BF16),
             pltpu.VMEM((2, 2, 4, 1, 128), jnp.int32),
             pltpu.VMEM((2, 4, 1, 128), jnp.int32),
-            pltpu.VMEM((5, 4, 8, 128), F32),
+            pltpu.VMEM((3, 8, 8, 128), F32),
+            pltpu.VMEM((ROWS, D), F32),
+            pltpu.VMEM((ROWS, 1), F32),
+            pltpu.VMEM((ROWS, D), F32),
+            pltpu.VMEM((ROWS, 1), F32),
             pltpu.VMEM((ROWS, D), BF16),
             pltpu.VMEM((ROWS, D), BF16),
             dma((2,)),
@@ -472,7 +474,7 @@
             dma((events,)), dma((events,)),
             dma((5,)), dma((5,)),
             dma((15,)), dma((15,)),
-            dma((5, 3)), dma((5, 3)),
+            dma((3, 7)), dma((3, 7)),
         ],
         compiler_params=pltpu.CompilerParams(
             collective_id=0, has_side_effects=True, vmem_limit_bytes=60 << 20

time: 62 us -> 61.6 us (level)
  no operation moved by 1% of the time
where the time goes in v4:
time: 61.6 us; the launch traced here: 61.4 us
  Pallas kernels  56.1 us (91%)
  between operations  3.62 us (6%)
  local copies, waits for them, and re-layouts  1.63 us (3%)
    pallas_call x1, Pallas kernels, on_device(): pl.pallas_call(kernel, out_shape=(pltpu.VMEM((ROWS, D), F32), pltpu.VMEM(...  56.1 us
    unnamed x2, local copies, waits for them, and re-layouts  1.63 us

profile of v4, /device:TPU:1, one launch (start us, length us, event | category | flops | bytes accessed | tf_op | source)
XLA Modules:
  0.0 61.4 jit_solution(201391493851091155)
XLA Ops:
  1.9 56.1 %pair_loss.1 = (f32[128,1152]{1,0:T(8,128)S(1)}, f32[128,1152]{1,0:T(8,128)S(1)}, f32[1]{0:T(128)}) custom-call(bf16[128,1152]{1,0:T(8,128)(2,1)} %img_hbm.1, bf16[128,1152]{1,0:T(8,128)(2,1)} %txt_hbm.1, s32[1,128]{1,0:T(1,128)} %bitcast.2, s32[1,128]{1,0:T(1,128)} %bitcast.3, f32[1]{0:T(128)S(6)} %copy.14.sharp_ref, f32[1]{0:T(128)S(6)} %copy.15.offset_ref), custom_call_target="tpu_custom_call" | custom-call | flops 14495514624 | bytes 2097152 | tf_op jit(solution)/shard_map/pair_loss/pallas_call | solution.py:435
  58.1 0.8 %copy.12 = f32[128,1152]{1,0:T(8,128)} copy(f32[128,1152]{1,0:T(8,128)S(1)} %get-tuple-element.3) | data formatting | bytes 1179648
  58.9 0.8 %copy.13 = f32[128,1152]{1,0:T(8,128)} copy(f32[128,1152]{1,0:T(8,128)S(1)} %get-tuple-element.4) | data formatting | bytes 1179648
